TPU v7x, 32 devices: a whole 2x2x4 slice. The times are simulated.
32 devices in a mesh: groups: 2 (over y), ctx: 4 (over z), dom: 2 (over x), tp: 2 (over core).
Axes of the slice: x: 2, y: 2, z: 4, core: 2. Of those that a mesh axis runs over, the one named last changes fastest.
Arguments:
- queries: bfloat16 [8, 32, 8, 8, 128], P('groups', 'dom', 'tp'), parts along dimension 0, may hold values from -8 to 8
- prompt_cache: bfloat16 [4, 8192, 8, 128], P('groups', 'ctx', 'tp'), parts along dimension 0, may hold values from -8 to 8
- suffix_cache: bfloat16 [4, 32, 16, 8, 128], P('groups', 'dom', 'ctx', 'tp'), parts along dimension 0, may hold values from -8 to 8
- new_kv: bfloat16 [8, 2, 32, 8, 128], P('groups', None, 'dom', 'tp'), parts along dimension 0, may hold values from -8 to 8
- ancestors: int32 [8, 32], P('groups'), parts along dimension 0, may hold values from 0 to 31, as said below
- lengths: int32 [64], P('groups'), parts along dimension 0, may hold values from 1 to 12, as said below
Outputs:
- attended: bfloat16 [8, 32, 8, 8, 128], P('groups', 'dom', 'tp'), parts along dimension 0
There are 2 independent parts, one for each index of `groups`. A program takes and returns all parts, laid end to end along the dimension named above; each array names one. Nothing has to cross between parts.
Inputs may be any that keep to these rules, and one draw needn't show every extreme that they name: `ancestors`: particle p is owned by owner p // 16. In every step, of the 16 offspring of one owner at most 16 have their ancestor among the particles of any one owner, and each owner has exactly 16 from some one owner. `lengths`: the largest length is reached in every draw.
All inputs are finite; a program needn't handle non-finite values.
Results may differ from a plain program's by a relative error of at most 0.005.
Values may be sent and summed in bfloat16 or wider, within the bound.
No kernel may reach another device: no remote copies, remote signals or barrier semaphores. Data moves between devices by JAX's collectives and lax.ppermute only.
A program may use at most 128 MiB of HBM per device.

v0:
```python
import functools
import math

import jax
import jax.numpy as jnp
from jax import lax
from jax.experimental import pallas as pl
from jax.experimental.pallas import tpu as pltpu
from jax.sharding import PartitionSpec as P

LANES = 128
HIDDEN = -1e30
NN = (((1,), (0,)), ((), ()))
NT = (((1,), (1,)), ((), ()))
SMALL = pl.CostEstimate(flops=0, bytes_accessed=4096, transcendentals=0)


def round_up(value, multiple):
    return -(-value // multiple) * multiple


def dot(a, b, dims):
    return lax.dot_general(a, b, dims, preferred_element_type=jnp.float32)


def eye_mask(rows):
    shape = (rows, LANES)
    return lax.broadcasted_iota(jnp.int32, shape, 0) == lax.broadcasted_iota(jnp.int32, shape, 1)


def column_to_lanes(column):
    rows = column.shape[0]
    block = min(rows, LANES)
    mask = eye_mask(block)
    return jnp.concatenate(
        [
            jnp.sum(jnp.where(mask, column[at : at + block], 0.0), axis=0, keepdims=True)
            for at in range(0, rows, block)
        ],
        axis=0,
    )


def lanes_to_column(lanes, rows):
    block = min(rows, LANES)
    mask = eye_mask(block)
    return jnp.concatenate(
        [
            jnp.sum(jnp.where(mask, lanes[i : i + 1], 0.0), axis=1, keepdims=True)
            for i in range(lanes.shape[0])
        ],
        axis=0,
    )


def tail_rows(rows):
    return round_up(3 * -(-rows // LANES), 16)


def message_shape(rows, size):
    return rows + tail_rows(rows), size


def pack_tail(column):
    lanes = column_to_lanes(column)
    high = lanes.astype(jnp.bfloat16).astype(jnp.float32)
    middle = (lanes - high).astype(jnp.bfloat16).astype(jnp.float32)
    low = lanes - high - middle
    parts = jnp.concatenate([high, middle, low], axis=0)
    spare = tail_rows(column.shape[0]) - parts.shape[0]
    return jnp.concatenate([parts, jnp.zeros((spare, LANES), jnp.float32)], axis=0).astype(
        jnp.bfloat16
    )


def unpack_tail(tail, rows):
    tail = tail.astype(jnp.float32)
    blocks = -(-rows // LANES)
    lanes = tail[:blocks] + tail[blocks : 2 * blocks] + tail[2 * blocks : 3 * blocks]
    return lanes_to_column(lanes, rows)


def in_hbm(array):
    return pltpu.with_memory_space_constraint(array, pltpu.HBM)


def message_kernel(
    heads, suffix_ref, new_ref, ancestors_ref, lengths_ref,
    out_ref, parents_ref, extents_ref, here, wide, sems,
):
    steps, each = new_ref.shape[0], new_ref.shape[2]
    total = here.shape[1]
    is_last = lax.axis_index("ctx") == lax.axis_size("ctx") - 1
    suffix_copy = pltpu.make_async_copy(suffix_ref, here, sems.at[0])
    token_copies = [
        pltpu.make_async_copy(
            new_ref.at[step], here.at[:, pl.ds(step * each, each)], sems.at[1 + step]
        )
        for step in range(steps)
    ]
    small = [
        pltpu.make_async_copy(ancestors_ref, parents_ref, sems.at[1 + steps]),
        pltpu.make_async_copy(lengths_ref, extents_ref, sems.at[2 + steps]),
    ]
    for copy in small:
        copy.start()

    @pl.when(is_last)
    def _():
        for copy in token_copies:
            copy.start()
        for copy in token_copies:
            copy.wait()

    @pl.when(jnp.logical_not(is_last))
    def _():
        suffix_copy.start()
        suffix_copy.wait()

    for kind in range(2):
        wide[kind] = here[kind].astype(jnp.float32)
        for head in range(heads):
            part = wide[kind, pl.ds(head, total // heads, stride=heads), :]
            out_ref[kind, head] = part.astype(out_ref.dtype)
    for copy in small:
        copy.wait()


def build_message(suffix, new, ancestors, lengths, heads):
    _, rows, size = suffix.shape
    lengths = lengths.reshape(1, -1)
    operands = (suffix, new, ancestors, lengths)
    return pl.pallas_call(
        functools.partial(message_kernel, heads),
        in_specs=[pl.BlockSpec(memory_space=pltpu.HBM)] * len(operands),
        out_shape=(
            jax.ShapeDtypeStruct((2, heads, rows // heads, size), suffix.dtype),
            jax.ShapeDtypeStruct(ancestors.shape, ancestors.dtype),
            jax.ShapeDtypeStruct(lengths.shape, lengths.dtype),
        ),
        scratch_shapes=[
            pltpu.VMEM(suffix.shape, suffix.dtype),
            pltpu.VMEM(suffix.shape, jnp.float32),
            pltpu.SemaphoreType.DMA((3 + new.shape[0],)),
        ],
        compiler_params=pltpu.CompilerParams(vmem_limit_bytes=24 << 20),
        cost_estimate=SMALL,
    )(*[in_hbm(operand) for operand in operands])


def iota(shape, axis):
    return lax.broadcasted_iota(jnp.int32, shape, axis)


def lineage_bias(ancestors_ref, lengths_ref, states, owners, suffix_dev):
    steps, particles = ancestors_ref.shape
    per_owner = particles // owners
    each = per_owner * suffix_dev
    my_owner = lax.axis_index("dom")
    my_shard = lax.axis_index("ctx")
    is_last = my_shard == lax.axis_size("ctx") - 1
    square = (particles, particles)
    same = iota(square, 0) == iota(square, 1)

    def as_column(row):
        return jnp.sum(jnp.where(same, row, 0), axis=1, keepdims=True)

    products = {}
    for step in range(steps):
        parent = as_column(ancestors_ref[step : step + 1, :])
        products[step - 1, step] = (parent == iota(square, 1)).astype(jnp.bfloat16)
    for length in range(2, steps + 1):
        for step in range(length - 1, steps):
            after = step - length
            middle = (step + after + 1) // 2
            both = dot(products[middle, step], products[after, middle], NN)
            products[after, step] = both.astype(jnp.bfloat16)
    for step in range(steps):
        states[step, :, :particles] = products[-1, step].astype(jnp.float32)
        for token in range(steps):
            here = slice((1 + token) * particles, (2 + token) * particles)
            if token < step:
                states[step, :, here] = products[token, step].astype(jnp.float32)
            else:
                states[step, :, here] = same.astype(jnp.float32) * float(token == step)
    rows = pl.ds(pl.multiple_of(my_owner * per_owner, per_owner), per_owner)
    mine = jnp.concatenate([states[step, rows, :] for step in range(steps)], axis=0)
    mine = mine.astype(jnp.bfloat16)
    lengths = as_column(lengths_ref[...])
    shape = (particles, owners * each)
    column = iota(shape, 1)
    source = column // each
    first = lax.rem(my_owner + owners - source, owners) * per_owner
    inner = column - source * each
    position = my_shard * suffix_dev + lax.rem(inner, suffix_dev)
    by_particle = iota(shape, 0) == first + inner // suffix_dev
    by_token = iota(shape, 0) == first + lax.rem(inner, per_owner)
    seen = [by_particle & (position < lengths) & jnp.logical_not(is_last)]
    seen += [by_token & (inner // per_owner == token) & is_last for token in range(steps)]
    table = jnp.concatenate([s.astype(jnp.bfloat16) for s in seen], axis=0)
    return jnp.where(dot(mine, table, NN) > 0.5, 0.0, HIDDEN)


def split_kernel(
    heads, block, owners, suffix_dev,
    rows_ref, parents_ref, extents_ref, *refs,
):
    out_refs = refs[: 2 * heads]
    bias_ref, here, wide, states, sems = refs[2 * heads :]
    total = out_refs[0].shape[0]
    places = [(kind, at) for kind in range(2) for at in range(0, total, block)]
    copies = [
        pltpu.make_async_copy(
            rows_ref.at[kind, pl.ds(at * heads, block * heads)],
            here.at[kind, pl.ds(at * heads, block * heads)],
            sems.at[i],
        )
        for i, (kind, at) in enumerate(places)
    ]
    for copy in copies:
        copy.start()
    bias_ref[...] = lineage_bias(parents_ref, extents_ref, states, owners, suffix_dev)
    for i, (kind, at) in enumerate(places):
        copies[i].wait()
        wide[i % 2] = here[kind, at * heads : (at + block) * heads].astype(jnp.float32)
        for head in range(heads):
            part = wide[i % 2, pl.ds(head, block, stride=heads), :]
            out_refs[kind * heads + head][at : at + block] = part.astype(rows_ref.dtype)


def split_prompt(rows, parents, extents, heads, owners, suffix_dev):
    total = rows.shape[1] // heads
    block = math.gcd(total, 512)
    size = rows.shape[2]
    steps, particles = parents.shape
    return pl.pallas_call(
        functools.partial(split_kernel, heads, block, owners, suffix_dev),
        in_specs=[pl.BlockSpec(memory_space=pltpu.HBM)]
        + [pl.BlockSpec(memory_space=pltpu.VMEM)] * 2,
        out_shape=(
            *[jax.ShapeDtypeStruct((total, size), rows.dtype)] * (2 * heads),
            jax.ShapeDtypeStruct(
                (steps * particles // owners, particles * suffix_dev), jnp.float32
            ),
        ),
        scratch_shapes=[
            pltpu.VMEM(rows.shape, rows.dtype),
            pltpu.VMEM((2, block * heads, size), jnp.float32),
            pltpu.VMEM((steps, particles, (1 + steps) * particles), jnp.float32),
            pltpu.SemaphoreType.DMA((2 * total // block,)),
        ],
        compiler_params=pltpu.CompilerParams(vmem_limit_bytes=24 << 20),
        cost_estimate=SMALL,
    )(in_hbm(rows), parents, extents)


def with_ones(values):
    return jnp.concatenate([values, jnp.ones_like(values)], axis=1)


def row_peak(scores):
    return jnp.max(scores, axis=1, keepdims=True)


def weigh(scores, factor, offset):
    return jnp.exp2(scores * factor - offset).astype(jnp.bfloat16)


def work_space(streams, rows, total, size):
    block = math.gcd(total, 512)
    return [
        pltpu.VMEM((3, rows, block), jnp.float32),
        pltpu.VMEM((streams, 2, rows, math.gcd(total, 2 * block)), jnp.bfloat16),
        pltpu.VMEM((streams * rows, 2 * size), jnp.float32),
    ]


def prompt_sum(streams, factor, scores, weights, sums):
    rows, total = streams[0][0].shape[0], streams[0][1].shape[0]
    block, wide = scores.shape[2], weights.shape[3]
    units = [(at, i) for at in range(0, total, block) for i in range(len(streams))]
    offsets = [None] * len(streams)

    def score(n):
        at, i = units[n]
        scores[n % 3] = dot(streams[i][0], streams[i][1][at : at + block], NT)

    def weight(n):
        at, i = units[n]
        if at == 0:
            top = row_peak(scores[n % 3])
            peak = streams[i][3]
            offsets[i] = (top if peak is None else jnp.maximum(top, peak)) * factor
        there = slice(at % wide, at % wide + block)
        weights[i, at // wide % 2, :, there] = weigh(scores[n % 3], factor, offsets[i])

    def gather(n):
        at, i = units[n]
        end = at + block
        if end % wide:
            return
        part = dot(weights[i, at // wide % 2], with_ones(streams[i][2][end - wide : end]), NN)
        here = slice(i * rows, (i + 1) * rows)
        sums[here] = part if end == wide else sums[here] + part

    score(0)
    score(1)
    for n in range(len(units)):
        if n + 2 < len(units):
            score(n + 2)
        weight(n)
        if n:
            gather(n - 1)
    gather(len(units) - 1)
    return offsets


def half_bit(level):
    shard = lax.axis_index("ctx")
    return lax.rem((shard >> level) + (shard >> (level + 1)), 2)


def first_step(q_ref, kept):
    bit = half_bit(0)
    return (bit if kept else 1 - bit) * (q_ref.shape[0] // 2)


def queries_of(q_ref, head, first, number):
    _, per_owner, _, group, size = q_ref.shape
    return q_ref[pl.ds(first, number), :, head].reshape(number * per_owner * group, size)


def prompt_kernel(heads, kept, factor, q_ref, *refs):
    k_refs, v_refs = refs[: len(heads)], refs[len(heads) : 2 * len(heads)]
    together_ref, offset_ref, scores, weights = refs[2 * len(heads) :]
    first, number = first_step(q_ref, kept), q_ref.shape[0] // 2
    streams = [
        (queries_of(q_ref, head, first, number), k_ref, v_ref, None)
        for head, k_ref, v_ref in zip(heads, k_refs, v_refs)
    ]
    offsets = prompt_sum(streams, factor, scores, weights, together_ref)
    offset = jnp.concatenate(offsets, axis=0)
    offset_ref[...] = jnp.broadcast_to(offset, offset_ref.shape)


def in_vmem(count, ordered=True):
    last = [pl.BlockSpec(memory_space=pl.ANY)] if ordered else []
    return [pl.BlockSpec(memory_space=pltpu.VMEM)] * count + last


def begin(queries, prompt, heads, kept, factor):
    steps, per_owner, _, group, size = queries.shape
    rows = steps * per_owner * group // 2
    keys, values = prompt
    space = work_space(len(heads), rows, keys[0].shape[0], size)
    return pl.pallas_call(
        functools.partial(prompt_kernel, heads, kept, factor),
        in_specs=in_vmem(1 + 2 * len(heads), False),
        out_shape=(
            jax.ShapeDtypeStruct((len(heads) * rows, 2 * size), jnp.float32),
            jax.ShapeDtypeStruct((len(heads) * rows, LANES), jnp.float32),
        ),
        scratch_shapes=space[:2],
        compiler_params=pltpu.CompilerParams(vmem_limit_bytes=24 << 20),
        cost_estimate=SMALL,
    )(queries, *[keys[head] for head in heads], *[values[head] for head in heads])


def attend_kernel(heads, kept, factor, owners, started, *refs):
    count = len(heads)
    q_ref, bias_ref = refs[:2]
    row_refs = refs[2 : 2 + owners]
    refs = refs[2 + owners :]
    k_refs, v_refs, refs = refs[:count], refs[count : 2 * count], refs[2 * count :]
    begun, refs = refs[: 2 * started], refs[2 * started + 1 :]
    if kept:
        out, log_sums, *work = refs
    else:
        send_ref, out, log_sums, *work = refs
    steps, per_owner, _, group, size = q_ref.shape
    columns = bias_ref.shape[1]
    number = steps // 2
    rows = number * per_owner * group
    start = first_step(q_ref, kept)

    def suffix_of(head, kind):
        return jnp.concatenate([ref[kind, head] for ref in row_refs], axis=0)

    def suffix_scores(q, head, first, number):
        at = pl.multiple_of(first * per_owner, per_owner)
        bias = bias_ref[pl.ds(at, number * per_owner), :]
        bias = jnp.broadcast_to(bias[:, None, :], (number * per_owner, group, columns))
        return dot(q, suffix_of(head, 0), NT) + bias.reshape(number * per_owner * group, columns)

    def store(i, at, together, offset):
        sums = together[:, size:]
        out[i, pl.ds(at, sums.shape[0]), :] = together[:, :size] / sums
        log_sums[i, pl.ds(at, sums.shape[0]), :] = offset + jnp.log2(sums)
        return sums

    queries = [queries_of(q_ref, head, start, number) for head in heads]
    extras = [suffix_scores(q, head, start, number) for q, head in zip(queries, heads)]
    if started:
        offsets = [begun[1][i * rows : (i + 1) * rows, :1] for i in range(count)]
        togethers = begun[0]
    else:
        streams = [(q, k, v, row_peak(e)) for q, k, v, e in zip(queries, k_refs, v_refs, extras)]
        offsets = prompt_sum(streams, factor, *work)
        togethers = work[-1]
    worst = []
    for i, head in enumerate(heads):
        weight = weigh(extras[i], factor, offsets[i])
        together = togethers[i * rows : (i + 1) * rows]
        together = together + dot(weight, with_ones(suffix_of(head, 1)), NN)
        worst.append(jnp.max(store(i, 0, together, offsets[i])))

    for i, head in enumerate(heads):

        @pl.when(jnp.logical_not(worst[i] < 2.0**100))
        def _():
            @pl.loop(0, number)
            def _(step):
                q = queries_of(q_ref, head, start + step, 1)
                extra = suffix_scores(q, head, start + step, 1)
                scores = dot(q, k_refs[i][...], NT)
                offset = jnp.maximum(row_peak(scores), row_peak(extra)) * factor
                weight = weigh(scores, factor, offset)
                together = dot(weight, with_ones(v_refs[i][...]), NN)
                weight = weigh(extra, factor, offset)
                together = together + dot(weight, with_ones(suffix_of(head, 1)), NN)
                here = per_owner * group
                store(i, pl.multiple_of(step * here, here), together, offset)

    if not kept:
        for i in range(count):
            send_ref[i * rows : (i + 1) * rows] = out[i].astype(jnp.bfloat16)
        column = jnp.concatenate([log_sums[i, :, :1] for i in range(count)], axis=0)
        send_ref[count * rows :] = pack_tail(column)


def attend(queries, prompt, bias, row_list, heads, kept, factor, begun, after):
    steps, per_owner, _, group, size = queries.shape
    rows = steps * per_owner * group // 2
    count = len(heads)
    keys, values = prompt
    operands = (
        queries, bias, *row_list,
        *[keys[head] for head in heads], *[values[head] for head in heads], *begun,
    )
    parts = [((count, rows, size), jnp.float32), ((count, rows, LANES), jnp.float32)]
    send = jax.ShapeDtypeStruct(message_shape(count * rows, size), jnp.bfloat16)
    space = work_space(count, rows, keys[0].shape[0], size)
    return pl.pallas_call(
        functools.partial(
            attend_kernel, heads, kept, factor, len(row_list), len(begun) // 2
        ),
        in_specs=in_vmem(len(operands)),
        out_shape=tuple(jax.ShapeDtypeStruct(*part) for part in parts) if kept else send,
        scratch_shapes=[*([] if kept else [pltpu.VMEM(*part) for part in parts]), *space],
        compiler_params=pltpu.CompilerParams(vmem_limit_bytes=32 << 20),
        cost_estimate=SMALL,
    )(*operands, after)


def merge(out_a, sum_a, out_b, sum_b):
    top = jnp.maximum(sum_a, sum_b)
    weight_a = jnp.exp2(sum_a - top)
    weight_b = jnp.exp2(sum_b - top)
    total = weight_a + weight_b
    return (out_a * weight_a + out_b * weight_b) / total, top + jnp.log2(total)


def merge_kernel(level, last, keep_ref, sums_ref, got_ref, _, *outs):
    count, rows = keep_ref.shape[:2]
    got_sums = unpack_tail(got_ref[count * rows :], count * rows)
    merged = []
    for i in range(count):
        here = slice(i * rows, (i + 1) * rows)
        got = got_ref[here].astype(jnp.float32)
        merged.append(merge(keep_ref[i], sums_ref[i][:, :1], got, got_sums[here]))
    part = rows if last else rows // 2
    bit = half_bit(level) == 1

    def choose(first, value):
        return value if last else jnp.where(first, value[:part], value[part:])

    send = outs[0]
    for i, (out, _) in enumerate(merged):
        send[i * part : (i + 1) * part] = choose(bit, out).astype(jnp.bfloat16)
    send[count * part :] = pack_tail(
        jnp.concatenate([choose(bit, log_sum) for _, log_sum in merged], axis=0)
    )
    if not last:
        _, keep, wide = outs
        for i, (out, log_sum) in enumerate(merged):
            keep[i] = choose(~bit, out)
            wide[i] = jnp.broadcast_to(choose(~bit, log_sum), (part, LANES))


def merge_parts(keep, sums, got, level, last, after):
    count, rows, size = keep.shape
    part = rows if last else rows // 2
    shapes = [jax.ShapeDtypeStruct(message_shape(count * part, size), jnp.bfloat16)]
    if not last:
        shapes.append(jax.ShapeDtypeStruct((count, part, size), jnp.float32))
        shapes.append(jax.ShapeDtypeStruct((count, part, LANES), jnp.float32))
    return pl.pallas_call(
        functools.partial(merge_kernel, level, last),
        in_specs=in_vmem(3),
        out_shape=tuple(shapes),
        compiler_params=pltpu.CompilerParams(vmem_limit_bytes=16 << 20),
        cost_estimate=SMALL,
    )(keep, sums, got, after)


def finish_kernel(mine_ref, got_ref, _, out_ref):
    count, rows = out_ref.shape[0], math.prod(out_ref.shape[1:-1])
    mine_sums = unpack_tail(mine_ref[count * rows :], count * rows)
    got_sums = unpack_tail(got_ref[count * rows :], count * rows)
    for i in range(count):
        here = slice(i * rows, (i + 1) * rows)
        out, _ = merge(
            mine_ref[here].astype(jnp.float32),
            mine_sums[here],
            got_ref[here].astype(jnp.float32),
            got_sums[here],
        )
        out_ref[i] = out.astype(jnp.bfloat16).reshape(out_ref.shape[1:])


def finish(mine, got, shape, after):
    return pl.pallas_call(
        finish_kernel,
        in_specs=in_vmem(2),
        out_shape=jax.ShapeDtypeStruct(shape, jnp.bfloat16),
        compiler_params=pltpu.CompilerParams(vmem_limit_bytes=16 << 20),
        cost_estimate=SMALL,
    )(mine, got, after)


def place_kernel(levels, plan, *refs):
    part_refs = refs[: len(plan)]
    out_ref, sems = refs[-2:]
    copies = []
    for (head, own), ref in zip(plan, part_refs):
        blocks = ref.shape[1]
        bit = half_bit(0)
        at = (bit if own else 1 - bit) * blocks
        for i in range(ref.shape[0]):
            there = out_ref.at[pl.ds(at, blocks), :, head + i]
            copies.append(pltpu.make_async_copy(ref.at[i], there, sems.at[len(copies)]))
    for copy in copies:
        copy.start()
    for copy in copies:
        copy.wait()


def place(out, parts, shape, levels, after):
    arrays = [array for array, _, _ in parts]
    plan = [(head, own) for _, head, own in parts]
    others = [after] if out is None else [after, out]
    return pl.pallas_call(
        functools.partial(place_kernel, levels, plan),
        in_specs=[pl.BlockSpec(memory_space=pltpu.VMEM)] * len(arrays)
        + [pl.BlockSpec(memory_space=pl.ANY), pl.BlockSpec(memory_space=pltpu.HBM)][: len(others)],
        out_specs=pl.BlockSpec(memory_space=pltpu.HBM),
        out_shape=pltpu.HBM(shape, jnp.bfloat16),
        input_output_aliases={} if out is None else {len(arrays) + 1: 0},
        scratch_shapes=[pltpu.SemaphoreType.DMA((sum(a.shape[0] for a in arrays),))],
        compiler_params=pltpu.CompilerParams(vmem_limit_bytes=16 << 20),
        cost_estimate=SMALL,
    )(*arrays, *others)


def on_device(shards, owners, queries, prompt_cache, suffix_cache, new_kv, ancestors, lengths):
    steps, per_owner, heads, group, size = queries.shape
    suffix_dev = suffix_cache.shape[2]
    factor = math.log2(math.e) / math.sqrt(size)
    levels = shards.bit_length() - 1
    if shards != 1 << levels or levels < 2 or steps % 2 or suffix_dev != steps:
        raise ValueError("unsupported sizes")

    def swap(value, bit):
        return lax.ppermute(value, "ctx", [(i, i ^ ((2 << bit) - 1)) for i in range(shards)])

    prompt_rows = prompt_cache.reshape(2, -1, size)
    mine, parents, extents = build_message(
        suffix_cache.reshape(2, -1, size),
        new_kv.reshape(steps, 2, -1, size),
        ancestors,
        lengths,
        heads,
    )
    row_list = [mine] + [
        lax.ppermute(mine, "dom", [(i, (i + hop) % owners) for i in range(owners)])
        for hop in range(1, owners)
    ]
    *prompt, bias = split_prompt(
        prompt_rows, parents, extents, heads, owners, suffix_dev
    )
    prompt = prompt[:heads], prompt[heads:]
    last = [bias]

    def follow(results):
        last[0] = results[0] if isinstance(results, (tuple, list)) else results
        return results

    messages = {}
    blocks = steps * per_owner >> (levels - 1)

    def run_attend(group, kept, begun=()):
        return follow(
            attend(queries, prompt, bias, row_list, group, kept, factor, begun, last[0])
        )

    def run_merges(got, parts):
        for level in range(1, levels):
            send, *parts = follow(merge_parts(*parts, got, level, level == levels - 1, last[0]))
            got = swap(send, level)
        return send, got

    parts = []

    def run_finish(count, send, got):
        return follow(finish(send, got, (count, blocks, group, size), last[0]))

    def run_gather(head, done):
        count = done.shape[0]
        for level in range(levels - 2, 0, -1):
            other = swap(done, level)
            done = jnp.where(
                half_bit(level) == 1,
                jnp.concatenate([other, done], axis=1),
                jnp.concatenate([done, other], axis=1),
            )
        done = done.reshape(count, steps // 2, per_owner, group, size)
        parts.append((done, head, True))
        parts.append((swap(done, 0), head, False))

    first = max(heads // 2, 1)
    groups = [tuple(range(heads))[at : at + first] for at in range(0, heads, first)]
    begun = follow(begin(queries, prompt, groups[0], False, factor))
    arrived, kept = [], []
    for number, one in enumerate(groups):
        arrived.append(swap(run_attend(one, False, () if number else begun), 0))
        if not number:
            kept.append(run_attend(one, True))
    pairs = []
    for number, one in enumerate(groups):
        if number:
            kept.append(run_attend(one, True))
        pairs.append(run_merges(arrived[number], kept[number]))
    for one, pair in zip(groups, pairs):
        run_gather(one[0], run_finish(len(one), *pair))
    late = parts[-1:]
    early = [part for part in parts if not any(part is one for one in late)]
    out = place(None, early, queries.shape, levels, last[0]) if early else None
    return place(out, late, queries.shape, levels, last[0])


def solution(mesh):
    return jax.shard_map(
        functools.partial(on_device, mesh.shape["ctx"], mesh.shape["dom"]),
        mesh=mesh,
        in_specs=(
            P("groups", "dom", "tp", None, None),
            P("groups", "ctx", "tp", None),
            P("groups", "dom", "ctx", "tp", None),
            P("groups", None, "dom", "tp", None),
            P("groups", None),
            P("groups"),
        ),
        out_specs=P("groups", "dom", "tp", None, None),
        check_vma=False,
    )
```

profile of v0, /device:TPU:20, one launch (start us, length us, event | category | flops | bytes accessed | tf_op | source)
XLA Modules:
  0.0 39.6 jit_solution(2113187947010256275)
XLA Ops:
  0.0 0.0 copy-start
  0.0 1.1 %shard_map.64 = (bf16[2,4,64,128]{3,2,1,0:T(8,128)(2,1)S(1)}, s32[4,32]{1,0:T(4,128)S(1)}, s32[1,32]{1,0:T(1,128)S(1)}) custom-call(bf16[2,256,128]{2,1,0:T(8,128)(2,1)} %bitcast.11, bf16[4,2,64,128]{3,2,1,0:T(8,128)(2,1)} %bitcast.12, s32[4,32]{1,0:T(4,128)} %ancestors_ref.1, s32[1,32]{1,0:T(1,128)} %bitcast.13), custom_call_target="tpu_custom_call" | custom-call | bytes 4096 | tf_op jit(solution)/shard_map/pallas_call | solution.py:133
  1.1 1.6 %collective-permute-start = (bf16[2,4,64,128]{3,2,1,0:T(8,128)(2,1)S(1)}, bf16[2,4,64,128]{3,2,1,0:T(8,128)(2,1)S(1)}, u32[]{:S(2)}, u32[]{:S(2)}) collective-permute-start(bf16[2,4,64,128]{3,2,1,0:T(8,128)(2,1)S(1)} %get-tuple-element.26.refs_2_), channel_id=1, source_target_pairs={{0,2},{2,0},{1,3},{3,1},{4,6},{6,4},{5,7},{7,5},{8,10},{10,8},{9,1... | collective-permute-start | bytes 393224 | tf_op jit(solution)/shard_map/ppermute | solution.py:595
  2.7 2.7 %shard_map.65 = (bf16[2048,128]{1,0:T(8,128)(2,1)S(1)}, bf16[2048,128]{1,0:T(8,128)(2,1)S(1)}, bf16[2048,128]{1,0:T(8,128)(2,1)S(1)}, bf16[2048,128]{1,0:T(8,128...) custom-call(bf16[2,8192,128]{2,1,0:T(8,128)(2,1)} %bitcast.10, ...), custom_call_target="tpu_custom_call" | custom-call | bytes 4096 | tf_op jit(solution)/shard_map/pallas_call | solution.py:236
  5.4 0.0 copy-done
  5.4 1.4 %shard_map.66 = (f32[512,256]{1,0:T(8,128)S(1)}, f32[512,128]{1,0:T(8,128)S(1)}) custom-call(bf16[4,16,4,8,128]{4,3,2,1,0:T(8,128)(2,1)S(1)} %copy-done, bf16[2048,128]{1,0:T(8,128)(2,1)S(1)} %get-tuple-element.31.refs_0_.refs_4_, bf16[2048,128]{1,0:T(8,128)(2,1)S(1)} %get-tuple-element.32.refs_1_.refs_5_, ...), custom_call_target="tpu_custom_call" | custom-call | bytes 4096 | tf_op jit(solution)/shard_map/pallas_call | solution.py:356
  6.8 0.0 collective-permute-done.refs_3_
  6.8 2.5 %shard_map.67.refs_8_ = bf16[528,128]{1,0:T(8,128)(2,1)S(1)} custom-call(bf16[4,16,4,8,128]{4,3,2,1,0:T(8,128)(2,1)S(1)} %copy-done, f32[64,128]{1,0:T(8,128)S(1)} %get-tuple-element.25.refs_1_, bf16[2,4,64,128]{3,2,1,0:T(8,128)(2,1)S(1)} %get-tuple-element.26.refs_2_, bf16[2,4,64,128]{3,2,1,0:T(8,128)(2,1)S(1)} %collective-permute-done.refs_3_, ...), custom_call_target="tpu_custom_call" | custom-call | bytes 4096 | tf_op jit(solution)/shard_map/pallas_call | solution.py:453
  9.3 1.5 %collective-permute-start.1 = (bf16[528,128]{1,0:T(8,128)(2,1)S(1)}, bf16[528,128]{1,0:T(8,128)(2,1)S(1)}, u32[]{:S(2)}, u32[]{:S(2)}) collective-permute-start(bf16[528,128]{1,0:T(8,128)(2,1)S(1)} %shard_map.67.refs_8_), channel_id=1, source_target_pairs={{0,4},{4,0},{8,12},{12,8},{1,5},{5,1},{9,13},{13,9},{2,6},{6,2},{1... | collective-permute-start | bytes 405512 | tf_op jit(solution)/shard_map/ppermute | solution.py:584
  10.9 3.4 %shard_map.68 = (f32[2,256,128]{2,1,0:T(8,128)S(1)}, f32[2,256,128]{2,1,0:T(8,128)S(1)}) custom-call(bf16[4,16,4,8,128]{4,3,2,1,0:T(8,128)(2,1)S(1)} %copy-done, f32[64,128]{1,0:T(8,128)S(1)} %get-tuple-element.25.refs_1_, bf16[2,4,64,128]{3,2,1,0:T(8,128)(2,1)S(1)} %get-tuple-element.26.refs_2_, bf16[2,4,64,128]{3,2,1,0:T(8,128)(2,1)S(1)} %collective-permute-done.refs_3_, ...), custom_call_target="tpu_custom_call" | custom-call | bytes 4096 | tf_op jit(solution)/shard_map/pallas_call | solution.py:453
  14.3 3.6 %shard_map.69._ = bf16[528,128]{1,0:T(8,128)(2,1)S(1)} custom-call(bf16[4,16,4,8,128]{4,3,2,1,0:T(8,128)(2,1)S(1)} %copy-done, f32[64,128]{1,0:T(8,128)S(1)} %get-tuple-element.25.refs_1_, bf16[2,4,64,128]{3,2,1,0:T(8,128)(2,1)S(1)} %get-tuple-element.26.refs_2_, bf16[2,4,64,128]{3,2,1,0:T(8,128)(2,1)S(1)} %collective-permute-done.refs_3_, ...), custom_call_target="tpu_custom_call" | custom-call | bytes 4096 | tf_op jit(solution)/shard_map/pallas_call | solution.py:453
  17.9 2.5 %collective-permute-start.2 = (bf16[528,128]{1,0:T(8,128)(2,1)S(1)}, bf16[528,128]{1,0:T(8,128)(2,1)S(1)}, u32[]{:S(2)}, u32[]{:S(2)}) collective-permute-start(bf16[528,128]{1,0:T(8,128)(2,1)S(1)} %shard_map.69._), channel_id=1, source_target_pairs={{0,4},{4,0},{8,12},{12,8},{1,5},{5,1},{9,13},{13,9},{2,6},{6,2},{1... | collective-permute-start | bytes 405512 | tf_op jit(solution)/shard_map/ppermute | solution.py:584
  20.4 0.0 collective-permute-done.1.got_ref
  20.4 0.5 %shard_map.70.refs_8_.mine_ref = bf16[528,128]{1,0:T(8,128)(2,1)S(1)} custom-call(f32[2,256,128]{2,1,0:T(8,128)S(1)} %get-tuple-element.37.refs_8_.keep_ref, f32[2,256,128]{2,1,0:T(8,128)S(1)} %get-tuple-element.38.sums_ref, bf16[528,128]{1,0:T(8,128)(2,1)S(1)} %collective-permute-done.1.got_ref, bf16[528,128]{1,0:T(8,128)(2,1)S(1)} %shard_map.69._), custom_call_target="tpu_custom_call" | custom-call | bytes 4096 | tf_op jit(solution)/shard_map/pallas_call | solution.py:507
  20.9 0.1 collective-permute-start.4
  21.0 3.7 %shard_map.71 = (f32[2,256,128]{2,1,0:T(8,128)S(1)}, f32[2,256,128]{2,1,0:T(8,128)S(1)}) custom-call(bf16[4,16,4,8,128]{4,3,2,1,0:T(8,128)(2,1)S(1)} %copy-done, f32[64,128]{1,0:T(8,128)S(1)} %get-tuple-element.25.refs_1_, bf16[2,4,64,128]{3,2,1,0:T(8,128)(2,1)S(1)} %get-tuple-element.26.refs_2_, bf16[2,4,64,128]{3,2,1,0:T(8,128)(2,1)S(1)} %collective-permute-done.refs_3_, ...), custom_call_target="tpu_custom_call" | custom-call | bytes 4096 | tf_op jit(solution)/shard_map/pallas_call | solution.py:453
  24.6 0.0 collective-permute-done.2.got_ref
  24.7 0.5 %shard_map.72._.mine_ref = bf16[528,128]{1,0:T(8,128)(2,1)S(1)} custom-call(f32[2,256,128]{2,1,0:T(8,128)S(1)} %get-tuple-element.39.keep_ref._, f32[2,256,128]{2,1,0:T(8,128)S(1)} %get-tuple-element.40.sums_ref, bf16[528,128]{1,0:T(8,128)(2,1)S(1)} %collective-permute-done.2.got_ref, f32[2,256,128]{2,1,0:T(8,128)S(1)} %get-tuple-element.39.keep_ref._), custom_call_target="tpu_custom_call" | custom-call | bytes 4096 | tf_op jit(solution)/shard_map/pallas_call | solution.py:507
  25.1 0.2 collective-permute-start.3
  25.3 4.9 %collective-permute-done.4.got_ref = bf16[528,128]{1,0:T(8,128)(2,1)S(1)} collective-permute-done((bf16[528,128]{1,0:T(8,128)(2,1)S(1)}, bf16[528,128]{1,0:T(8,128)(2,1)S(1)}, u32[]{:S(2)}, u32[]{:S(2)}) %collective-permute-start.4) | collective-permute-done | bytes 135200 | tf_op jit(solution)/shard_map/ppermute | solution.py:584
  30.2 0.5 %shard_map.73._ = bf16[2,32,8,128]{3,2,1,0:T(8,128)(2,1)S(1)} custom-call(bf16[528,128]{1,0:T(8,128)(2,1)S(1)} %shard_map.70.refs_8_.mine_ref, bf16[528,128]{1,0:T(8,128)(2,1)S(1)} %collective-permute-done.4.got_ref, bf16[528,128]{1,0:T(8,128)(2,1)S(1)} %shard_map.72._.mine_ref), custom_call_target="tpu_custom_call" | custom-call | bytes 4096 | tf_op jit(solution)/shard_map/pallas_call | solution.py:532
  30.7 0.1 collective-permute-start.6
  30.8 2.4 %collective-permute-done.3.got_ref = bf16[528,128]{1,0:T(8,128)(2,1)S(1)} collective-permute-done((bf16[528,128]{1,0:T(8,128)(2,1)S(1)}, bf16[528,128]{1,0:T(8,128)(2,1)S(1)}, u32[]{:S(2)}, u32[]{:S(2)}) %collective-permute-start.3) | collective-permute-done | bytes 135200 | tf_op jit(solution)/shard_map/ppermute | solution.py:584
  33.2 0.5 %shard_map.74.refs_3_.refs_1_ = bf16[2,32,8,128]{3,2,1,0:T(8,128)(2,1)S(1)} custom-call(bf16[528,128]{1,0:T(8,128)(2,1)S(1)} %shard_map.72._.mine_ref, bf16[528,128]{1,0:T(8,128)(2,1)S(1)} %collective-permute-done.3.got_ref, bf16[2,32,8,128]{3,2,1,0:T(8,128)(2,1)S(1)} %shard_map.73._), custom_call_target="tpu_custom_call" | custom-call | bytes 4096 | tf_op jit(solution)/shard_map/pallas_call | solution.py:532
  33.7 0.9 %collective-permute-start.5 = (bf16[2,2,16,8,128]{4,3,2,1,0:T(8,128)(2,1)S(1)}, bf16[2,2,16,8,128]{4,3,2,1,0:T(8,128)(2,1)S(1)}, u32[]{:S(2)}, u32[]{:S(2)}) collective-permute-start(bf16[2,2,16,8,128]{4,3,2,1,0:T(8,128)(2,1)S(1)} %bitcast.6), channel_id=1, source_target_pairs={{0,4},{4,0},{8,12},{12,8},{1,5},{5,1},{9,13},{13,9},{2,6},{6,2},{1... | collective-permute-start | bytes 393224 | tf_op jit(solution)/shard_map/ppermute | solution.py:584
  34.6 1.9 %collective-permute-done.6.refs_1_ = bf16[2,2,16,8,128]{4,3,2,1,0:T(8,128)(2,1)S(1)} collective-permute-done((bf16[2,2,16,8,128]{4,3,2,1,0:T(8,128)(2,1)S(1)}, bf16[2,2,16,8,128]{4,3,2,1,0:T(8,128)(2,1)S(1)}, u32[]{:S(2)}, u32[]{:S(2)}) %collective-permute-start.6) | collective-permute-done | bytes 131104 | tf_op jit(solution)/shard_map/ppermute | solution.py:584
  36.5 0.8 %shard_map.75.refs_2_ = bf16[4,16,4,8,128]{4,3,2,1,0:T(8,128)(2,1)} custom-call(bf16[2,2,16,8,128]{4,3,2,1,0:T(8,128)(2,1)S(1)} %bitcast.9, bf16[2,2,16,8,128]{4,3,2,1,0:T(8,128)(2,1)S(1)} %collective-permute-done.6.refs_1_, bf16[2,2,16,8,128]{4,3,2,1,0:T(8,128)(2,1)S(1)} %bitcast.7, bf16[2,32,8,128]{3,2,1,0:T(8,128)(2,1)S(1)} %shard_map.74.refs_3_.refs_1_), custom_call_target="tpu_custom_call" | custom-call | bytes 4096 | tf_op jit(solution)/shard_map/pallas_call | solution.py:562
  37.3 1.5 %collective-permute-done.5.refs_0_ = bf16[2,2,16,8,128]{4,3,2,1,0:T(8,128)(2,1)S(1)} collective-permute-done((bf16[2,2,16,8,128]{4,3,2,1,0:T(8,128)(2,1)S(1)}, bf16[2,2,16,8,128]{4,3,2,1,0:T(8,128)(2,1)S(1)}, u32[]{:S(2)}, u32[]{:S(2)}) %collective-permute-start.5) | collective-permute-done | bytes 131104 | tf_op jit(solution)/shard_map/ppermute | solution.py:584
  38.7 0.7 %shard_map.76 = bf16[4,16,4,8,128]{4,3,2,1,0:T(8,128)(2,1)} custom-call(bf16[2,2,16,8,128]{4,3,2,1,0:T(8,128)(2,1)S(1)} %collective-permute-done.5.refs_0_, bf16[2,32,8,128]{3,2,1,0:T(8,128)(2,1)S(1)} %shard_map.74.refs_3_.refs_1_, bf16[4,16,4,8,128]{4,3,2,1,0:T(8,128)(2,1)} %shard_map.75.refs_2_), custom_call_target="tpu_custom_call", output_to_operand_aliasing={{}: (2, {})} | custom-call | bytes 4096 | tf_op jit(solution)/shard_map/pallas_call | solution.py:562
Async XLA Ops:
  0.0 5.4 %copy-start = (bf16[4,16,4,8,128]{4,3,2,1,0:T(8,128)(2,1)S(1)}, bf16[4,16,4,8,128]{4,3,2,1,0:T(8,128)(2,1)}, u32[]{:S(2)}) copy-start(bf16[4,16,4,8,128]{4,3,2,1,0:T(8,128)(2,1)} %refs_0_.7) | copy-start | bytes 1572868
  1.1 5.7 %collective-permute-start = (bf16[2,4,64,128]{3,2,1,0:T(8,128)(2,1)S(1)}, bf16[2,4,64,128]{3,2,1,0:T(8,128)(2,1)S(1)}, u32[]{:S(2)}, u32[]{:S(2)}) collective-permute-start(bf16[2,4,64,128]{3,2,1,0:T(8,128)(2,1)S(1)} %get-tuple-element.26.refs_2_), channel_id=1, source_target_pairs={{0,2},{2,0},{1,3},{3,1},{4,6},{6,4},{5,7},{7,5},{8,10},{10,8},{9,1... | collective-permute-start | bytes 393224 | tf_op jit(solution)/shard_map/ppermute | solution.py:595
  9.3 11.1 %collective-permute-start.1 = (bf16[528,128]{1,0:T(8,128)(2,1)S(1)}, bf16[528,128]{1,0:T(8,128)(2,1)S(1)}, u32[]{:S(2)}, u32[]{:S(2)}) collective-permute-start(bf16[528,128]{1,0:T(8,128)(2,1)S(1)} %shard_map.67.refs_8_), channel_id=1, source_target_pairs={{0,4},{4,0},{8,12},{12,8},{1,5},{5,1},{9,13},{13,9},{2,6},{6,2},{1... | collective-permute-start | bytes 405512 | tf_op jit(solution)/shard_map/ppermute | solution.py:584
  17.9 6.7 %collective-permute-start.2 = (bf16[528,128]{1,0:T(8,128)(2,1)S(1)}, bf16[528,128]{1,0:T(8,128)(2,1)S(1)}, u32[]{:S(2)}, u32[]{:S(2)}) collective-permute-start(bf16[528,128]{1,0:T(8,128)(2,1)S(1)} %shard_map.69._), channel_id=1, source_target_pairs={{0,4},{4,0},{8,12},{12,8},{1,5},{5,1},{9,13},{13,9},{2,6},{6,2},{1... | collective-permute-start | bytes 405512 | tf_op jit(solution)/shard_map/ppermute | solution.py:584
  20.9 9.3 %collective-permute-start.4 = (bf16[528,128]{1,0:T(8,128)(2,1)S(1)}, bf16[528,128]{1,0:T(8,128)(2,1)S(1)}, u32[]{:S(2)}, u32[]{:S(2)}) collective-permute-start(bf16[528,128]{1,0:T(8,128)(2,1)S(1)} %shard_map.70.refs_8_.mine_ref), channel_id=1, source_target_pairs={{0,12},{4,8},{8,4},{12,0},{1,13},{5,9},{9,5},{13,1},{2,14},{6,10},... | collective-permute-start | bytes 405512 | tf_op jit(solution)/shard_map/ppermute | solution.py:584
  25.1 8.1 %collective-permute-start.3 = (bf16[528,128]{1,0:T(8,128)(2,1)S(1)}, bf16[528,128]{1,0:T(8,128)(2,1)S(1)}, u32[]{:S(2)}, u32[]{:S(2)}) collective-permute-start(bf16[528,128]{1,0:T(8,128)(2,1)S(1)} %shard_map.72._.mine_ref), channel_id=1, source_target_pairs={{0,12},{4,8},{8,4},{12,0},{1,13},{5,9},{9,5},{13,1},{2,14},{6,10},... | collective-permute-start | bytes 405512 | tf_op jit(solution)/shard_map/ppermute | solution.py:584
  30.7 5.8 %collective-permute-start.6 = (bf16[2,2,16,8,128]{4,3,2,1,0:T(8,128)(2,1)S(1)}, bf16[2,2,16,8,128]{4,3,2,1,0:T(8,128)(2,1)S(1)}, u32[]{:S(2)}, u32[]{:S(2)}) collective-permute-start(bf16[2,2,16,8,128]{4,3,2,1,0:T(8,128)(2,1)S(1)} %bitcast.8), channel_id=1, source_target_pairs={{0,4},{4,0},{8,12},{12,8},{1,5},{5,1},{9,13},{13,9},{2,6},{6,2},{1... | collective-permute-start | bytes 393224 | tf_op jit(solution)/shard_map/ppermute | solution.py:584
  33.7 5.0 %collective-permute-start.5 = (bf16[2,2,16,8,128]{4,3,2,1,0:T(8,128)(2,1)S(1)}, bf16[2,2,16,8,128]{4,3,2,1,0:T(8,128)(2,1)S(1)}, u32[]{:S(2)}, u32[]{:S(2)}) collective-permute-start(bf16[2,2,16,8,128]{4,3,2,1,0:T(8,128)(2,1)S(1)} %bitcast.6), channel_id=1, source_target_pairs={{0,4},{4,0},{8,12},{12,8},{1,5},{5,1},{9,13},{13,9},{2,6},{6,2},{1... | collective-permute-start | bytes 393224 | tf_op jit(solution)/shard_map/ppermute | solution.py:584
where the time goes:
time: 40.2 us; the launch traced here: 39.6 us
  Pallas kernels  21.7 us (54%)
  waiting for transfers between devices  10.7 us (27%)
  starting transfers between devices  6.8 us (17%)
    pallas_call x4, Pallas kernels, attend(): pl.pallas_call(functools.partial(attend_kernel, heads, kept, factor, len(...  13.2 us
    ppermute x6, waiting for transfers between devices, swap(): lax.ppermute(value, 'ctx', [(i, i ^ (2 << bit) - 1) for i in range(shards)])  10.7 us
    ppermute x6, starting transfers between devices, swap(): lax.ppermute(value, 'ctx', [(i, i ^ (2 << bit) - 1) for i in range(shards)])  5.24 us
    pallas_call x1, Pallas kernels, split_prompt(): pl.pallas_call(functools.partial(split_kernel, heads, block, owners, suff...  2.68 us
    ppermute x1, starting transfers between devices, on_device(): lax.ppermute(mine, 'dom', [(i, (i + hop) % owners) for i in range(owners)])  1.56 us
    pallas_call x2, Pallas kernels, place(): pl.pallas_call(functools.partial(place_kernel, levels, plan), in_specs=[p...  1.45 us
    pallas_call x1, Pallas kernels, begin(): pl.pallas_call(functools.partial(prompt_kernel, heads, kept, factor), in_...  1.41 us
    pallas_call x1, Pallas kernels, build_message(): pl.pallas_call(functools.partial(message_kernel, heads), in_specs=[pl.Blo...  1.1 us
  transfers between devices with their start and end apart: 7, of which 4 were waited for; matrix products, arithmetic and copies ran while one was open for 0% of the time, Pallas kernels for 44%

commit v1 on v0

--- a/solution.py
+++ b/solution.py
@@ -85,8 +85,8 @@
 
 
 def message_kernel(
-    heads, suffix_ref, new_ref, ancestors_ref, lengths_ref,
-    out_ref, parents_ref, extents_ref, here, wide, sems,
+    heads, suffix_ref, new_ref, ancestors_ref, lengths_ref, prompt_ref,
+    out_ref, parents_ref, extents_ref, keys_ref, here, wide, sems,
 ):
     steps, each = new_ref.shape[0], new_ref.shape[2]
     total = here.shape[1]
@@ -101,20 +101,22 @@
     small = [
         pltpu.make_async_copy(ancestors_ref, parents_ref, sems.at[1 + steps]),
         pltpu.make_async_copy(lengths_ref, extents_ref, sems.at[2 + steps]),
+        pltpu.make_async_copy(
+            prompt_ref.at[0, pl.ds(0, keys_ref.shape[0])], keys_ref, sems.at[3 + steps]
+        ),
     ]
-    for copy in small:
-        copy.start()
 
     @pl.when(is_last)
     def _():
-        for copy in token_copies:
+        for copy in token_copies + small:
             copy.start()
         for copy in token_copies:
             copy.wait()
 
     @pl.when(jnp.logical_not(is_last))
     def _():
-        suffix_copy.start()
+        for copy in [suffix_copy] + small:
+            copy.start()
         suffix_copy.wait()
 
     for kind in range(2):
@@ -126,10 +128,10 @@
         copy.wait()
 
 
-def build_message(suffix, new, ancestors, lengths, heads):
+def build_message(suffix, new, ancestors, lengths, prompt, heads, ahead):
     _, rows, size = suffix.shape
     lengths = lengths.reshape(1, -1)
-    operands = (suffix, new, ancestors, lengths)
+    operands = (suffix, new, ancestors, lengths, prompt)
     return pl.pallas_call(
         functools.partial(message_kernel, heads),
         in_specs=[pl.BlockSpec(memory_space=pltpu.HBM)] * len(operands),
@@ -137,11 +139,12 @@
             jax.ShapeDtypeStruct((2, heads, rows // heads, size), suffix.dtype),
             jax.ShapeDtypeStruct(ancestors.shape, ancestors.dtype),
             jax.ShapeDtypeStruct(lengths.shape, lengths.dtype),
+            jax.ShapeDtypeStruct((ahead, size), prompt.dtype),
         ),
         scratch_shapes=[
             pltpu.VMEM(suffix.shape, suffix.dtype),
             pltpu.VMEM(suffix.shape, jnp.float32),
-            pltpu.SemaphoreType.DMA((3 + new.shape[0],)),
+            pltpu.SemaphoreType.DMA((4 + new.shape[0],)),
         ],
         compiler_params=pltpu.CompilerParams(vmem_limit_bytes=24 << 20),
         cost_estimate=SMALL,
@@ -203,12 +206,13 @@
 
 def split_kernel(
     heads, block, owners, suffix_dev,
-    rows_ref, parents_ref, extents_ref, *refs,
+    rows_ref, keys_ref, parents_ref, extents_ref, *refs,
 ):
     out_refs = refs[: 2 * heads]
     bias_ref, here, wide, states, sems = refs[2 * heads :]
     total = out_refs[0].shape[0]
     places = [(kind, at) for kind in range(2) for at in range(0, total, block)]
+    ahead = keys_ref.shape[0] // (heads * block)
     copies = [
         pltpu.make_async_copy(
             rows_ref.at[kind, pl.ds(at * heads, block * heads)],
@@ -217,18 +221,22 @@
         )
         for i, (kind, at) in enumerate(places)
     ]
-    for copy in copies:
+    for copy in copies[ahead:]:
         copy.start()
     bias_ref[...] = lineage_bias(parents_ref, extents_ref, states, owners, suffix_dev)
     for i, (kind, at) in enumerate(places):
-        copies[i].wait()
-        wide[i % 2] = here[kind, at * heads : (at + block) * heads].astype(jnp.float32)
+        there = slice(at * heads, (at + block) * heads)
+        if i < ahead:
+            wide[i % 2] = keys_ref[there].astype(jnp.float32)
+        else:
+            copies[i].wait()
+            wide[i % 2] = here[kind, there].astype(jnp.float32)
         for head in range(heads):
             part = wide[i % 2, pl.ds(head, block, stride=heads), :]
             out_refs[kind * heads + head][at : at + block] = part.astype(rows_ref.dtype)
 
 
-def split_prompt(rows, parents, extents, heads, owners, suffix_dev):
+def split_prompt(rows, keys, parents, extents, heads, owners, suffix_dev):
     total = rows.shape[1] // heads
     block = math.gcd(total, 512)
     size = rows.shape[2]
@@ -236,7 +244,7 @@
     return pl.pallas_call(
         functools.partial(split_kernel, heads, block, owners, suffix_dev),
         in_specs=[pl.BlockSpec(memory_space=pltpu.HBM)]
-        + [pl.BlockSpec(memory_space=pltpu.VMEM)] * 2,
+        + [pl.BlockSpec(memory_space=pltpu.VMEM)] * 3,
         out_shape=(
             *[jax.ShapeDtypeStruct((total, size), rows.dtype)] * (2 * heads),
             jax.ShapeDtypeStruct(
@@ -251,7 +259,7 @@
         ],
         compiler_params=pltpu.CompilerParams(vmem_limit_bytes=24 << 20),
         cost_estimate=SMALL,
-    )(in_hbm(rows), parents, extents)
+    )(in_hbm(rows), keys, parents, extents)
 
 
 def with_ones(values):
@@ -376,7 +384,7 @@
     if kept:
         out, log_sums, *work = refs
     else:
-        send_ref, out, log_sums, *work = refs
+        send_ref, log_sums, *work = refs
     steps, per_owner, _, group, size = q_ref.shape
     columns = bias_ref.shape[1]
     number = steps // 2
@@ -394,7 +402,12 @@
 
     def store(i, at, together, offset):
         sums = together[:, size:]
-        out[i, pl.ds(at, sums.shape[0]), :] = together[:, :size] / sums
+        result = together[:, :size] / sums
+        if kept:
+            out[i, pl.ds(at, sums.shape[0]), :] = result
+        else:
+            there = pl.ds(pl.multiple_of(i * rows + at, LANES), sums.shape[0])
+            send_ref[there, :] = result.astype(jnp.bfloat16)
         log_sums[i, pl.ds(at, sums.shape[0]), :] = offset + jnp.log2(sums)
         return sums
 
@@ -432,8 +445,6 @@
                 store(i, pl.multiple_of(step * here, here), together, offset)
 
     if not kept:
-        for i in range(count):
-            send_ref[i * rows : (i + 1) * rows] = out[i].astype(jnp.bfloat16)
         column = jnp.concatenate([log_sums[i, :, :1] for i in range(count)], axis=0)
         send_ref[count * rows :] = pack_tail(column)
 
@@ -456,7 +467,7 @@
         ),
         in_specs=in_vmem(len(operands)),
         out_shape=tuple(jax.ShapeDtypeStruct(*part) for part in parts) if kept else send,
-        scratch_shapes=[*([] if kept else [pltpu.VMEM(*part) for part in parts]), *space],
+        scratch_shapes=[*([] if kept else [pltpu.VMEM(*parts[1])]), *space],
         compiler_params=pltpu.CompilerParams(vmem_limit_bytes=32 << 20),
         cost_estimate=SMALL,
     )(*operands, after)
@@ -584,19 +595,21 @@
         return lax.ppermute(value, "ctx", [(i, i ^ ((2 << bit) - 1)) for i in range(shards)])
 
     prompt_rows = prompt_cache.reshape(2, -1, size)
-    mine, parents, extents = build_message(
+    mine, parents, extents, keys = build_message(
         suffix_cache.reshape(2, -1, size),
         new_kv.reshape(steps, 2, -1, size),
         ancestors,
         lengths,
+        prompt_rows,
         heads,
+        math.gcd(prompt_rows.shape[1] // 4, 1024 * heads),
     )
     row_list = [mine] + [
         lax.ppermute(mine, "dom", [(i, (i + hop) % owners) for i in range(owners)])
         for hop in range(1, owners)
     ]
     *prompt, bias = split_prompt(
-        prompt_rows, parents, extents, heads, owners, suffix_dev
+        prompt_rows, keys, parents, extents, heads, owners, suffix_dev
     )
     prompt = prompt[:heads], prompt[heads:]
     last = [bias]

time: 40.2 us -> 40.7 us (1.012)
  the two profiles are of different devices: /device:TPU:20 before, /device:TPU:0 now
where the time goes in v1:
time: 40.7 us; the launch traced here: 39.9 us
  Pallas kernels  17.7 us (43%)
  starting transfers between devices  15.4 us (38%)
  waiting for transfers between devices  6.64 us (16%)
    ppermute x6, starting transfers between devices, swap(): lax.ppermute(value, 'ctx', [(i, i ^ (2 << bit) - 1) for i in range(shards)])  12.4 us
    pallas_call x4, Pallas kernels, attend(): pl.pallas_call(functools.partial(attend_kernel, heads, kept, factor, len(...  9.45 us
    ppermute x6, waiting for transfers between devices, swap(): lax.ppermute(value, 'ctx', [(i, i ^ (2 << bit) - 1) for i in range(shards)])  6.64 us
    ppermute x1, starting transfers between devices, on_device(): lax.ppermute(mine, 'dom', [(i, (i + hop) % owners) for i in range(owners)])  3 us
    pallas_call x1, Pallas kernels, split_prompt(): pl.pallas_call(functools.partial(split_kernel, heads, block, owners, suff...  2.25 us
    pallas_call x2, Pallas kernels, place(): pl.pallas_call(functools.partial(place_kernel, levels, plan), in_specs=[p...  1.45 us
    pallas_call x1, Pallas kernels, begin(): pl.pallas_call(functools.partial(prompt_kernel, heads, kept, factor), in_...  1.41 us
    pallas_call x1, Pallas kernels, build_message(): pl.pallas_call(functools.partial(message_kernel, heads), in_specs=[pl.Blo...  1.26 us
  transfers between devices with their start and end apart: 7, of which 3 were waited for; matrix products, arithmetic and copies ran while one was open for 0% of the time, Pallas kernels for 33%

profile of v1, /device:TPU:0, one launch (start us, length us, event | category | flops | bytes accessed | tf_op | source)
XLA Modules:
  0.0 39.9 jit_solution(16596919876521760507)
XLA Ops:
  0.0 0.0 copy-start
  0.0 1.3 %shard_map.64 = (bf16[2,4,64,128]{3,2,1,0:T(8,128)(2,1)S(1)}, s32[4,32]{1,0:T(4,128)S(1)}, s32[1,32]{1,0:T(1,128)S(1)}, bf16[2048,128]{1,0:T(8,128)(2,1)S(1)}) custom-call(bf16[2,256,128]{2,1,0:T(8,128)(2,1)} %bitcast.12, bf16[4,2,64,128]{3,2,1,0:T(8,128)(2,1)} %bitcast.13, s32[4,32]{1,0:T(4,128)} %ancestors_ref.1, s32[1,32]{1,0:T(1,128)} %bitcast.14, ...), custom_call_target="tpu_custom_call" | custom-call | bytes 4096 | tf_op jit(solution)/shard_map/pallas_call | solution.py:135
  1.3 3.0 %collective-permute-start = (bf16[2,4,64,128]{3,2,1,0:T(8,128)(2,1)S(1)}, bf16[2,4,64,128]{3,2,1,0:T(8,128)(2,1)S(1)}, u32[]{:S(2)}, u32[]{:S(2)}) collective-permute-start(bf16[2,4,64,128]{3,2,1,0:T(8,128)(2,1)S(1)} %get-tuple-element.28.refs_2_), channel_id=1, source_target_pairs={{0,2},{2,0},{1,3},{3,1},{4,6},{6,4},{5,7},{7,5},{8,10},{10,8},{9,1... | collective-permute-start | bytes 393224 | tf_op jit(solution)/shard_map/ppermute | solution.py:608
  4.3 2.3 %shard_map.65 = (bf16[2048,128]{1,0:T(8,128)(2,1)S(1)}, bf16[2048,128]{1,0:T(8,128)(2,1)S(1)}, bf16[2048,128]{1,0:T(8,128)(2,1)S(1)}, bf16[2048,128]{1,0:T(8,128...) custom-call(bf16[2,8192,128]{2,1,0:T(8,128)(2,1)} %bitcast.11, ...), custom_call_target="tpu_custom_call" | custom-call | bytes 4096 | tf_op jit(solution)/shard_map/pallas_call | solution.py:244
  6.5 0.0 copy-done
  6.6 1.4 %shard_map.66 = (f32[512,256]{1,0:T(8,128)S(1)}, f32[512,128]{1,0:T(8,128)S(1)}) custom-call(bf16[4,16,4,8,128]{4,3,2,1,0:T(8,128)(2,1)S(1)} %copy-done, bf16[2048,128]{1,0:T(8,128)(2,1)S(1)} %get-tuple-element.33.refs_0_.refs_4_, bf16[2048,128]{1,0:T(8,128)(2,1)S(1)} %get-tuple-element.34.refs_1_.refs_5_, ...), custom_call_target="tpu_custom_call" | custom-call | bytes 4096 | tf_op jit(solution)/shard_map/pallas_call | solution.py:364
  8.0 0.0 collective-permute-done.refs_3_
  8.0 2.5 %shard_map.67.refs_8_ = bf16[528,128]{1,0:T(8,128)(2,1)S(1)} custom-call(bf16[4,16,4,8,128]{4,3,2,1,0:T(8,128)(2,1)S(1)} %copy-done, f32[64,128]{1,0:T(8,128)S(1)} %get-tuple-element.27.refs_1_, bf16[2,4,64,128]{3,2,1,0:T(8,128)(2,1)S(1)} %get-tuple-element.28.refs_2_, bf16[2,4,64,128]{3,2,1,0:T(8,128)(2,1)S(1)} %collective-permute-done.refs_3_, ...), custom_call_target="tpu_custom_call" | custom-call | bytes 4096 | tf_op jit(solution)/shard_map/pallas_call | solution.py:464
  10.5 1.7 %collective-permute-start.1 = (bf16[528,128]{1,0:T(8,128)(2,1)S(1)}, bf16[528,128]{1,0:T(8,128)(2,1)S(1)}, u32[]{:S(2)}, u32[]{:S(2)}) collective-permute-start(bf16[528,128]{1,0:T(8,128)(2,1)S(1)} %shard_map.67.refs_8_), channel_id=1, source_target_pairs={{0,4},{4,0},{8,12},{12,8},{1,5},{5,1},{9,13},{13,9},{2,6},{6,2},{1... | collective-permute-start | bytes 405512 | tf_op jit(solution)/shard_map/ppermute | solution.py:595
  12.2 3.4 %shard_map.68 = (f32[2,256,128]{2,1,0:T(8,128)S(1)}, f32[2,256,128]{2,1,0:T(8,128)S(1)}) custom-call(bf16[4,16,4,8,128]{4,3,2,1,0:T(8,128)(2,1)S(1)} %copy-done, f32[64,128]{1,0:T(8,128)S(1)} %get-tuple-element.27.refs_1_, bf16[2,4,64,128]{3,2,1,0:T(8,128)(2,1)S(1)} %get-tuple-element.28.refs_2_, bf16[2,4,64,128]{3,2,1,0:T(8,128)(2,1)S(1)} %collective-permute-done.refs_3_, ...), custom_call_target="tpu_custom_call" | custom-call | bytes 4096 | tf_op jit(solution)/shard_map/pallas_call | solution.py:464
  15.6 1.7 %shard_map.69._ = bf16[528,128]{1,0:T(8,128)(2,1)S(1)} custom-call(bf16[4,16,4,8,128]{4,3,2,1,0:T(8,128)(2,1)S(1)} %copy-done, f32[64,128]{1,0:T(8,128)S(1)} %get-tuple-element.27.refs_1_, bf16[2,4,64,128]{3,2,1,0:T(8,128)(2,1)S(1)} %get-tuple-element.28.refs_2_, bf16[2,4,64,128]{3,2,1,0:T(8,128)(2,1)S(1)} %collective-permute-done.refs_3_, ...), custom_call_target="tpu_custom_call" | custom-call | bytes 4096 | tf_op jit(solution)/shard_map/pallas_call | solution.py:464
  17.4 2.4 %collective-permute-start.2 = (bf16[528,128]{1,0:T(8,128)(2,1)S(1)}, bf16[528,128]{1,0:T(8,128)(2,1)S(1)}, u32[]{:S(2)}, u32[]{:S(2)}) collective-permute-start(bf16[528,128]{1,0:T(8,128)(2,1)S(1)} %shard_map.69._), channel_id=1, source_target_pairs={{0,4},{4,0},{8,12},{12,8},{1,5},{5,1},{9,13},{13,9},{2,6},{6,2},{1... | collective-permute-start | bytes 405512 | tf_op jit(solution)/shard_map/ppermute | solution.py:595
  19.7 0.0 collective-permute-done.1.got_ref
  19.7 0.5 %shard_map.70.refs_8_.mine_ref = bf16[528,128]{1,0:T(8,128)(2,1)S(1)} custom-call(f32[2,256,128]{2,1,0:T(8,128)S(1)} %get-tuple-element.39.refs_8_.keep_ref, f32[2,256,128]{2,1,0:T(8,128)S(1)} %get-tuple-element.40.sums_ref, bf16[528,128]{1,0:T(8,128)(2,1)S(1)} %collective-permute-done.1.got_ref, bf16[528,128]{1,0:T(8,128)(2,1)S(1)} %shard_map.69._), custom_call_target="tpu_custom_call" | custom-call | bytes 4096 | tf_op jit(solution)/shard_map/pallas_call | solution.py:518
  20.2 1.9 %collective-permute-start.4 = (bf16[528,128]{1,0:T(8,128)(2,1)S(1)}, bf16[528,128]{1,0:T(8,128)(2,1)S(1)}, u32[]{:S(2)}, u32[]{:S(2)}) collective-permute-start(bf16[528,128]{1,0:T(8,128)(2,1)S(1)} %shard_map.70.refs_8_.mine_ref), channel_id=1, source_target_pairs={{0,12},{4,8},{8,4},{12,0},{1,13},{5,9},{9,5},{13,1},{2,14},{6,10},... | collective-permute-start | bytes 405512 | tf_op jit(solution)/shard_map/ppermute | solution.py:595
  22.1 1.8 %shard_map.71 = (f32[2,256,128]{2,1,0:T(8,128)S(1)}, f32[2,256,128]{2,1,0:T(8,128)S(1)}) custom-call(bf16[4,16,4,8,128]{4,3,2,1,0:T(8,128)(2,1)S(1)} %copy-done, f32[64,128]{1,0:T(8,128)S(1)} %get-tuple-element.27.refs_1_, bf16[2,4,64,128]{3,2,1,0:T(8,128)(2,1)S(1)} %get-tuple-element.28.refs_2_, bf16[2,4,64,128]{3,2,1,0:T(8,128)(2,1)S(1)} %collective-permute-done.refs_3_, ...), custom_call_target="tpu_custom_call" | custom-call | bytes 4096 | tf_op jit(solution)/shard_map/pallas_call | solution.py:464
  23.8 0.0 collective-permute-done.2.got_ref
  23.8 0.5 %shard_map.72._.mine_ref = bf16[528,128]{1,0:T(8,128)(2,1)S(1)} custom-call(f32[2,256,128]{2,1,0:T(8,128)S(1)} %get-tuple-element.41.keep_ref._, f32[2,256,128]{2,1,0:T(8,128)S(1)} %get-tuple-element.42.sums_ref, bf16[528,128]{1,0:T(8,128)(2,1)S(1)} %collective-permute-done.2.got_ref, f32[2,256,128]{2,1,0:T(8,128)S(1)} %get-tuple-element.41.keep_ref._), custom_call_target="tpu_custom_call" | custom-call | bytes 4096 | tf_op jit(solution)/shard_map/pallas_call | solution.py:518
  24.3 2.1 %collective-permute-start.3 = (bf16[528,128]{1,0:T(8,128)(2,1)S(1)}, bf16[528,128]{1,0:T(8,128)(2,1)S(1)}, u32[]{:S(2)}, u32[]{:S(2)}) collective-permute-start(bf16[528,128]{1,0:T(8,128)(2,1)S(1)} %shard_map.72._.mine_ref), channel_id=1, source_target_pairs={{0,12},{4,8},{8,4},{12,0},{1,13},{5,9},{9,5},{13,1},{2,14},{6,10},... | collective-permute-start | bytes 405512 | tf_op jit(solution)/shard_map/ppermute | solution.py:595
  26.4 2.0 %collective-permute-done.4.got_ref = bf16[528,128]{1,0:T(8,128)(2,1)S(1)} collective-permute-done((bf16[528,128]{1,0:T(8,128)(2,1)S(1)}, bf16[528,128]{1,0:T(8,128)(2,1)S(1)}, u32[]{:S(2)}, u32[]{:S(2)}) %collective-permute-start.4) | collective-permute-done | bytes 135200 | tf_op jit(solution)/shard_map/ppermute | solution.py:595
  28.4 0.5 %shard_map.73._ = bf16[2,32,8,128]{3,2,1,0:T(8,128)(2,1)S(1)} custom-call(bf16[528,128]{1,0:T(8,128)(2,1)S(1)} %shard_map.70.refs_8_.mine_ref, bf16[528,128]{1,0:T(8,128)(2,1)S(1)} %collective-permute-done.4.got_ref, bf16[528,128]{1,0:T(8,128)(2,1)S(1)} %shard_map.72._.mine_ref), custom_call_target="tpu_custom_call" | custom-call | bytes 4096 | tf_op jit(solution)/shard_map/pallas_call | solution.py:543
  28.9 0.1 collective-permute-start.6
  29.0 2.3 %collective-permute-done.3.got_ref = bf16[528,128]{1,0:T(8,128)(2,1)S(1)} collective-permute-done((bf16[528,128]{1,0:T(8,128)(2,1)S(1)}, bf16[528,128]{1,0:T(8,128)(2,1)S(1)}, u32[]{:S(2)}, u32[]{:S(2)}) %collective-permute-start.3) | collective-permute-done | bytes 135200 | tf_op jit(solution)/shard_map/ppermute | solution.py:595
  31.3 0.5 %shard_map.74.refs_3_.refs_1_ = bf16[2,32,8,128]{3,2,1,0:T(8,128)(2,1)S(1)} custom-call(bf16[528,128]{1,0:T(8,128)(2,1)S(1)} %shard_map.72._.mine_ref, bf16[528,128]{1,0:T(8,128)(2,1)S(1)} %collective-permute-done.3.got_ref, bf16[2,32,8,128]{3,2,1,0:T(8,128)(2,1)S(1)} %shard_map.73._), custom_call_target="tpu_custom_call" | custom-call | bytes 4096 | tf_op jit(solution)/shard_map/pallas_call | solution.py:543
  31.8 4.2 %collective-permute-start.5 = (bf16[2,2,16,8,128]{4,3,2,1,0:T(8,128)(2,1)S(1)}, bf16[2,2,16,8,128]{4,3,2,1,0:T(8,128)(2,1)S(1)}, u32[]{:S(2)}, u32[]{:S(2)}) collective-permute-start(bf16[2,2,16,8,128]{4,3,2,1,0:T(8,128)(2,1)S(1)} %bitcast.6), channel_id=1, source_target_pairs={{0,4},{4,0},{8,12},{12,8},{1,5},{5,1},{9,13},{13,9},{2,6},{6,2},{1... | collective-permute-start | bytes 393224 | tf_op jit(solution)/shard_map/ppermute | solution.py:595
  36.0 0.0 collective-permute-done.6.refs_1_
  36.0 0.8 %shard_map.75.refs_2_ = bf16[4,16,4,8,128]{4,3,2,1,0:T(8,128)(2,1)} custom-call(bf16[2,2,16,8,128]{4,3,2,1,0:T(8,128)(2,1)S(1)} %bitcast.9, bf16[2,2,16,8,128]{4,3,2,1,0:T(8,128)(2,1)S(1)} %collective-permute-done.6.refs_1_, bf16[2,2,16,8,128]{4,3,2,1,0:T(8,128)(2,1)S(1)} %bitcast.7, bf16[2,32,8,128]{3,2,1,0:T(8,128)(2,1)S(1)} %shard_map.74.refs_3_.refs_1_), custom_call_target="tpu_custom_call" | custom-call | bytes 4096 | tf_op jit(solution)/shard_map/pallas_call | solution.py:573
  36.8 2.3 %collective-permute-done.5.refs_0_ = bf16[2,2,16,8,128]{4,3,2,1,0:T(8,128)(2,1)S(1)} collective-permute-done((bf16[2,2,16,8,128]{4,3,2,1,0:T(8,128)(2,1)S(1)}, bf16[2,2,16,8,128]{4,3,2,1,0:T(8,128)(2,1)S(1)}, u32[]{:S(2)}, u32[]{:S(2)}) %collective-permute-start.5) | collective-permute-done | bytes 131104 | tf_op jit(solution)/shard_map/ppermute | solution.py:595
  39.1 0.7 %shard_map.76 = bf16[4,16,4,8,128]{4,3,2,1,0:T(8,128)(2,1)} custom-call(bf16[2,2,16,8,128]{4,3,2,1,0:T(8,128)(2,1)S(1)} %collective-permute-done.5.refs_0_, bf16[2,32,8,128]{3,2,1,0:T(8,128)(2,1)S(1)} %shard_map.74.refs_3_.refs_1_, bf16[4,16,4,8,128]{4,3,2,1,0:T(8,128)(2,1)} %shard_map.75.refs_2_), custom_call_target="tpu_custom_call", output_to_operand_aliasing={{}: (2, {})} | custom-call | bytes 4096 | tf_op jit(solution)/shard_map/pallas_call | solution.py:573
Async XLA Ops:
  0.0 6.5 %copy-start = (bf16[4,16,4,8,128]{4,3,2,1,0:T(8,128)(2,1)S(1)}, bf16[4,16,4,8,128]{4,3,2,1,0:T(8,128)(2,1)}, u32[]{:S(2)}) copy-start(bf16[4,16,4,8,128]{4,3,2,1,0:T(8,128)(2,1)} %refs_0_.7) | copy-start | bytes 1572868
  1.3 6.7 %collective-permute-start = (bf16[2,4,64,128]{3,2,1,0:T(8,128)(2,1)S(1)}, bf16[2,4,64,128]{3,2,1,0:T(8,128)(2,1)S(1)}, u32[]{:S(2)}, u32[]{:S(2)}) collective-permute-start(bf16[2,4,64,128]{3,2,1,0:T(8,128)(2,1)S(1)} %get-tuple-element.28.refs_2_), channel_id=1, source_target_pairs={{0,2},{2,0},{1,3},{3,1},{4,6},{6,4},{5,7},{7,5},{8,10},{10,8},{9,1... | collective-permute-start | bytes 393224 | tf_op jit(solution)/shard_map/ppermute | solution.py:608
  10.5 9.2 %collective-permute-start.1 = (bf16[528,128]{1,0:T(8,128)(2,1)S(1)}, bf16[528,128]{1,0:T(8,128)(2,1)S(1)}, u32[]{:S(2)}, u32[]{:S(2)}) collective-permute-start(bf16[528,128]{1,0:T(8,128)(2,1)S(1)} %shard_map.67.refs_8_), channel_id=1, source_target_pairs={{0,4},{4,0},{8,12},{12,8},{1,5},{5,1},{9,13},{13,9},{2,6},{6,2},{1... | collective-permute-start | bytes 405512 | tf_op jit(solution)/shard_map/ppermute | solution.py:595
  17.4 6.5 %collective-permute-start.2 = (bf16[528,128]{1,0:T(8,128)(2,1)S(1)}, bf16[528,128]{1,0:T(8,128)(2,1)S(1)}, u32[]{:S(2)}, u32[]{:S(2)}) collective-permute-start(bf16[528,128]{1,0:T(8,128)(2,1)S(1)} %shard_map.69._), channel_id=1, source_target_pairs={{0,4},{4,0},{8,12},{12,8},{1,5},{5,1},{9,13},{13,9},{2,6},{6,2},{1... | collective-permute-start | bytes 405512 | tf_op jit(solution)/shard_map/ppermute | solution.py:595
  20.2 8.2 %collective-permute-start.4 = (bf16[528,128]{1,0:T(8,128)(2,1)S(1)}, bf16[528,128]{1,0:T(8,128)(2,1)S(1)}, u32[]{:S(2)}, u32[]{:S(2)}) collective-permute-start(bf16[528,128]{1,0:T(8,128)(2,1)S(1)} %shard_map.70.refs_8_.mine_ref), channel_id=1, source_target_pairs={{0,12},{4,8},{8,4},{12,0},{1,13},{5,9},{9,5},{13,1},{2,14},{6,10},... | collective-permute-start | bytes 405512 | tf_op jit(solution)/shard_map/ppermute | solution.py:595
  24.3 7.0 %collective-permute-start.3 = (bf16[528,128]{1,0:T(8,128)(2,1)S(1)}, bf16[528,128]{1,0:T(8,128)(2,1)S(1)}, u32[]{:S(2)}, u32[]{:S(2)}) collective-permute-start(bf16[528,128]{1,0:T(8,128)(2,1)S(1)} %shard_map.72._.mine_ref), channel_id=1, source_target_pairs={{0,12},{4,8},{8,4},{12,0},{1,13},{5,9},{9,5},{13,1},{2,14},{6,10},... | collective-permute-start | bytes 405512 | tf_op jit(solution)/shard_map/ppermute | solution.py:595
  28.9 7.1 %collective-permute-start.6 = (bf16[2,2,16,8,128]{4,3,2,1,0:T(8,128)(2,1)S(1)}, bf16[2,2,16,8,128]{4,3,2,1,0:T(8,128)(2,1)S(1)}, u32[]{:S(2)}, u32[]{:S(2)}) collective-permute-start(bf16[2,2,16,8,128]{4,3,2,1,0:T(8,128)(2,1)S(1)} %bitcast.8), channel_id=1, source_target_pairs={{0,4},{4,0},{8,12},{12,8},{1,5},{5,1},{9,13},{13,9},{2,6},{6,2},{1... | collective-permute-start | bytes 393224 | tf_op jit(solution)/shard_map/ppermute | solution.py:595
  31.8 7.4 %collective-permute-start.5 = (bf16[2,2,16,8,128]{4,3,2,1,0:T(8,128)(2,1)S(1)}, bf16[2,2,16,8,128]{4,3,2,1,0:T(8,128)(2,1)S(1)}, u32[]{:S(2)}, u32[]{:S(2)}) collective-permute-start(bf16[2,2,16,8,128]{4,3,2,1,0:T(8,128)(2,1)S(1)} %bitcast.6), channel_id=1, source_target_pairs={{0,4},{4,0},{8,12},{12,8},{1,5},{5,1},{9,13},{13,9},{2,6},{6,2},{1... | collective-permute-start | bytes 393224 | tf_op jit(solution)/shard_map/ppermute | solution.py:595
